TPU v7x, 512 devices: a whole 4x8x8 slice. The times are simulated.
512 devices in a mesh: tiles: 128 (over y, z, core), pairs: 4 (over x).
Axes of the slice: x: 4, y: 8, z: 8, core: 2. Of those that a mesh axis runs over, the one named last changes fastest.
Arguments:
- amplitudes: bfloat16 [32, 16384], P(None, 'tiles'), may hold values from -6 to 6
- integrals: bfloat16 [128, 4, 96, 128, 128], P('tiles', 'pairs'), may hold values from -0.02734375 to 0.02734375
- block_owner: int32 [128, 4, 96, 1], P('tiles', 'pairs'), may hold values from 0 to 127; in each aligned block of 96 rows (0 to 95, 96 to 191, ..., all dimensions but the last counted through in order) no two rows name the same one
- tile_dims: int32 [128], P('tiles'), may hold values from 1 to 128, as said below
- energy_gap: float32 [32, 16384], P('pairs', 'tiles'), may hold values from 0.5 to 4
Outputs:
- residual: float32 [32, 16384], P('pairs', 'tiles')
- updated: bfloat16 [32, 16384], P('pairs', 'tiles')
Inputs may be any that keep to these rules, and one draw needn't show every extreme that they name: `block_owner`: within one tile's list in one sub-slice the 96 named tiles are distinct. `tile_dims`: columns of a tile at or beyond its entry are padding; some tile is full.
All inputs are finite; a program needn't handle non-finite values.
Results may differ from a plain program's by a relative error of at most 0.0095.
Values may be sent and summed in bfloat16 or wider, within the bound.
A program may use at most 64 MiB of HBM per device.

v0:
```python
import jax
import jax.numpy as jnp
from jax import lax
from jax.sharding import PartitionSpec as P


def contract_sources(masked, pieces):
    number = pieces.shape[0]
    grouped = pieces.reshape((8, number // 8) + pieces.shape[1:])

    def group_product(group):
        return jnp.einsum("rc,nkc->nrk", masked, group, preferred_element_type=jnp.float32).astype(
            jnp.bfloat16
        )

    result = lax.map(group_product, grouped)
    return result.reshape((number,) + result.shape[2:])


def per_device(amplitudes, integrals, block_owner, tile_dims, energy_gap):
    tile_width = amplitudes.shape[1]
    own_count = energy_gap.shape[0]
    columns = lax.broadcasted_iota(jnp.int32, (1, tile_width), 1)
    live_columns = columns < tile_dims[0]
    masked = jnp.where(live_columns, amplitudes, jnp.zeros_like(amplitudes))
    blocks = integrals[0, 0]
    owners = block_owner[0, 0, :, 0]
    number = lax.axis_size("tiles")
    outgoing = jnp.zeros((number,) + blocks.shape[1:], blocks.dtype).at[owners].set(blocks)
    partials = contract_sources(
        masked, lax.all_to_all(outgoing, "tiles", split_axis=0, concat_axis=0, tiled=True)
    )
    returned = lax.all_to_all(partials, "tiles", split_axis=0, concat_axis=0, tiled=True)
    local_sum = jnp.sum(returned, axis=0, dtype=jnp.float32)
    residual = lax.psum_scatter(local_sum, "pairs", scatter_dimension=0, tiled=True)
    residual = jnp.where(live_columns, residual, jnp.zeros_like(residual))
    first_row = lax.axis_index("pairs") * own_count
    own_rows = lax.dynamic_slice_in_dim(masked, first_row, own_count, 0)
    updated = (own_rows.astype(jnp.float32) - residual / energy_gap).astype(jnp.bfloat16)
    return (residual, updated)


def solution(mesh):
    in_specs = (
        P(None, "tiles"),
        P("tiles", "pairs", None, None, None),
        P("tiles", "pairs", None, None),
        P("tiles"),
        P("pairs", "tiles"),
    )
    out_specs = (P("pairs", "tiles"), P("pairs", "tiles"))
    return jax.shard_map(
        per_device, mesh=mesh, in_specs=in_specs, out_specs=out_specs, check_vma=False
    )
```

profile of v0, /device:TPU:8, one launch (start us, length us, event | category | flops | bytes accessed | tf_op | source)
XLA Modules:
  0.0 212.8 jit_solution(11844531312116027651)
XLA Ops:
  0.6 0.0 copy-start
  0.6 0.8 fusion.6
  1.4 3.0 %broadcast_in_dim.35 = bf16[128,128,128]{2,1,0:T(8,128)(2,1)} broadcast(bf16[]{:T(256)} %constant.3.clone.1), dimensions={} | broadcast | bytes 4194306 | tf_op jit(solution)/shard_map/broadcast_in_dim | solution.py:29
  4.5 0.0 copy-done
  4.5 12.6 %scatter_fusion = bf16[128,128,128]{2,1,0:T(8,128)(2,1)} fusion(bf16[128,128,128]{2,1,0:T(8,128)(2,1)} %broadcast_in_dim.35, s32[96]{0:T(128)S(1)} %fusion.6, bf16[96,128,128]{2,1,0:T(8,128)(2,1)S(1)} %bitcast.28), kind=kCustom, calls=%fused_computation | custom fusion | bytes 9437568 | tf_op jit(solution)/shard_map/scatter | solution.py:29
  17.1 0.0 copy-start.1
  17.1 18.0 %all-to-all-start = ((bf16[128,128,128]{2,1,0:T(8,128)(2,1)}), bf16[128,128,128]{2,1,0:T(8,128)(2,1)}, u32[]{:S(2)}, u32[]{:S(2)}) async-start(bf16[128,128,128]{2,1,0:T(8,128)(2,1)} %scatter_fusion), calls=%async_computation | async-start | bytes 8388608 | tf_op jit(solution)/shard_map/all_to_all | solution.py:31
  35.1 0.0 copy-start.2
  35.8 0.0 copy-done.1
  35.8 95.6 %all-to-all-done = bf16[128,128,128]{2,1,0:T(8,128)(2,1)} async-done(((bf16[128,128,128]{2,1,0:T(8,128)(2,1)}), bf16[128,128,128]{2,1,0:T(8,128)(2,1)}, u32[]{:S(2)}, u32[]{:S(2)}) %all-to-all-start) | async-done | bytes 4194336 | tf_op jit(solution)/shard_map/all_to_all | solution.py:31
  131.5 15.8 %while.10 = (s32[]{:T(128)}, bf16[8,16,32,128]{3,2,1,0:T(8,128)(2,1)}, bf16[8,16,128,128]{3,2,1,0:T(8,128)(2,1)}, bf16[32,128]{1,0:T(8,128)(2,1)S(1)}, s32[]{:T(128)}) while((s32[]{:T(128)}, bf16[8,16,32,128]{3,2,1,0:T(8,128)(2,1)}, bf16[8,16,128,128]{3,2,1,0:T(8,128)(2,1)}, bf16[32,128]{1,0:T(8,128)(2,1)S(1)}, s32[]{:T(128)}) %tuple.23), condition=%wide.region_2.3_spmd, body=%wide.region_1.2_spmd.sunk | while | flops 16842752 | bytes 664637 | solution.py:16
  131.5 2.0 fusion.12
  133.4 2.0 fusion.12
  135.4 2.0 fusion.12
  137.4 2.0 fusion.12
  139.4 2.0 fusion.12
  141.3 2.0 fusion.12
  143.3 2.0 fusion.12
  145.3 2.0 fusion.12
  147.3 16.5 %all-to-all-start.1 = ((bf16[128,32,128]{2,1,0:T(8,128)(2,1)}), bf16[128,32,128]{2,1,0:T(8,128)(2,1)S(1)}, u32[]{:S(2)}, u32[]{:S(2)}) async-start(bf16[128,32,128]{2,1,0:T(8,128)(2,1)} %bitcast.9), calls=%async_computation.1 | async-start | bytes 2097152 | tf_op jit(solution)/shard_map/all_to_all | solution.py:33
  163.7 1.3 dynamic-slice
  165.7 29.4 %all-to-all-done.1 = bf16[128,32,128]{2,1,0:T(8,128)(2,1)S(1)} async-done(((bf16[128,32,128]{2,1,0:T(8,128)(2,1)}), bf16[128,32,128]{2,1,0:T(8,128)(2,1)S(1)}, u32[]{:S(2)}, u32[]{:S(2)}) %all-to-all-start.1) | async-done | bytes 1048608 | tf_op jit(solution)/shard_map/all_to_all | solution.py:33
  195.1 0.2 convert_reduce_fusion
  195.3 16.9 %all-reduce = f32[32,128]{1,0:T(8,128)S(1)} all-reduce(f32[32,128]{1,0:T(8,128)S(1)} %convert_reduce_fusion), channel_id=2, replica_groups=mesh['tiles'=128,'pairs'=4] {'pairs'}, use_global_device_ids=true, to_apply=%region_4.5.clone | all-reduce | flops 4096 | bytes 32768
  212.2 0.0 copy-done.2
  212.2 0.6 subtract_convert_fusion
  (3 shorter events, 0.0 us)
Async XLA Ops:
  0.6 3.8 %copy-start = (bf16[1,1,96,128,128]{4,3,2,1,0:T(8,128)(2,1)S(1)}, bf16[1,1,96,128,128]{4,3,2,1,0:T(8,128)(2,1)}, u32[]{:S(2)}) copy-start(bf16[1,1,96,128,128]{4,3,2,1,0:T(8,128)(2,1)} %param.8) | copy-start | bytes 9437188
  17.1 18.7 %copy-start.1 = (bf16[32,128]{1,0:T(8,128)(2,1)S(1)}, bf16[32,128]{1,0:T(8,128)(2,1)}, u32[]{:S(2)}) copy-start(bf16[32,128]{1,0:T(8,128)(2,1)} %param.7) | copy-start | bytes 24580
  17.1 114.4 %all-to-all-start = ((bf16[128,128,128]{2,1,0:T(8,128)(2,1)}), bf16[128,128,128]{2,1,0:T(8,128)(2,1)}, u32[]{:S(2)}, u32[]{:S(2)}) async-start(bf16[128,128,128]{2,1,0:T(8,128)(2,1)} %scatter_fusion), calls=%async_computation | async-start | bytes 8388608 | tf_op jit(solution)/shard_map/all_to_all | solution.py:31
  35.1 177.0 %copy-start.2 = (f32[8,128]{1,0:T(8,128)S(1)}, f32[8,128]{1,0:T(8,128)}, u32[]{:S(2)}) copy-start(f32[8,128]{1,0:T(8,128)} %param.11) | copy-start | bytes 12292
  147.3 47.8 %all-to-all-start.1 = ((bf16[128,32,128]{2,1,0:T(8,128)(2,1)}), bf16[128,32,128]{2,1,0:T(8,128)(2,1)S(1)}, u32[]{:S(2)}, u32[]{:S(2)}) async-start(bf16[128,32,128]{2,1,0:T(8,128)(2,1)} %bitcast.9), calls=%async_computation.1 | async-start | bytes 2097152 | tf_op jit(solution)/shard_map/all_to_all | solution.py:33
where the time goes:
time: 214 us; the launch traced here: 213 us
  waiting for transfers between devices  125 us (58%)
  starting transfers between devices  34.5 us (16%)
  local copies, waits for them, and re-layouts  16.9 us (8%)
  blocking collectives  16.9 us (8%)
  matrix products  15.8 us (7%)
    all_to_all x1, waiting for transfers between devices, per_device(): lax.all_to_all(outgoing, 'tiles', split_axis=0, concat_axis=0, tiled=True)  95.6 us
    all_to_all x1, waiting for transfers between devices, per_device(): lax.all_to_all(partials, 'tiles', split_axis=0, concat_axis=0, tiled=True)  29.4 us
    all_to_all x1, starting transfers between devices, per_device(): lax.all_to_all(outgoing, 'tiles', split_axis=0, concat_axis=0, tiled=True)  18 us
    unnamed x1, blocking collectives  16.9 us
    all_to_all x1, starting transfers between devices, per_device(): lax.all_to_all(partials, 'tiles', split_axis=0, concat_axis=0, tiled=True)  16.5 us
    dot_general x8, matrix products, group_product(): jnp.einsum('rc,nkc->nrk', masked, group, preferred_element_type=jnp.float32)  15.8 us
    scatter x1, local copies, waits for them, and re-layouts, per_device(): jnp.zeros((number,) + blocks.shape[1:], blocks.dtype).at[owners].set(blocks)  12.6 us
  transfers between devices with their start and end apart: 2, of which 2 were waited for; matrix products, arithmetic and copies ran while one was open for 1% of the time, Pallas kernels for 0%

commit v1 on v0

v1 whole, which is shorter than its diff:
```python
import jax
import jax.numpy as jnp
from jax import lax
from jax.experimental import pallas as pl
from jax.experimental.pallas import tpu as pltpu
from jax.sharding import PartitionSpec as P

RING = 8
HALF = RING // 2
GROUP = 2
GROUPS = HALF // GROUP
CHUNKS = 4
STEPS = (4, 3, 5, 2, 6, 1, 7)
NT_DIMS = (((1,), (1,)), ((), ()))


def kernel(
    owners_in,
    dims_in,
    amplitudes,
    integrals,
    energy_gap,
    out,
    owners,
    dims,
    raw,
    gap,
    blocks,
    mine,
    mine_wide,
    gathered,
    entry_rows,
    entries,
    terms,
    arrived,
    load_sems,
    entry_sems,
    partner_send,
    partner_recv,
    first_send,
    first_recv,
    second_send,
    second_recv,
    sum_send,
    sum_recv,
):
    tile = lax.axis_index("tiles")
    pair = lax.axis_index("pairs")
    pairs = lax.axis_size("pairs")
    core = tile % 2
    z = (tile // 2) % RING
    y = tile // (2 * RING)
    kind = (y + z) % 2
    partner = tile + 1 - 2 * core
    count = blocks.shape[1] - 1
    part = count // CHUNKS

    def along_z(step):
        return (y * RING + (z + step) % RING) * 2 + core

    def along_y(step):
        return (((y + step) % RING) * RING + z) * 2 + core

    load_raw = pltpu.make_async_copy(amplitudes, raw, load_sems.at[0])
    load_dims = pltpu.make_async_copy(dims_in, dims, load_sems.at[1])
    load_owners = pltpu.make_async_copy(owners_in, owners, load_sems.at[2])
    load_gap = pltpu.make_async_copy(energy_gap, gap, load_sems.at[3])
    load_raw.start()
    load_dims.start()

    barrier = pltpu.get_barrier_semaphore()
    for step in STEPS:
        pl.semaphore_signal(barrier, inc=1, device_id={"tiles": along_z(step)})
        pl.semaphore_signal(barrier, inc=1, device_id={"tiles": along_y(step)})
    for step in range(1, pairs):
        other = (pair + step) % pairs
        pl.semaphore_signal(barrier, inc=1, device_id={"pairs": other})
        pl.semaphore_signal(barrier, inc=1, device_id={"tiles": partner, "pairs": other})
    pl.semaphore_signal(barrier, inc=1, device_id={"tiles": partner})

    load_owners.start()
    load_gap.start()
    load_blocks = []
    for i in range(CHUNKS):
        rows = pl.ds(i * part, part)
        load = pltpu.make_async_copy(
            integrals.at[0, 0, rows], blocks.at[0, rows], load_sems.at[4 + i]
        )
        load.start()
        load_blocks.append(load)
    blocks[0, count] = jnp.zeros(blocks.shape[2:], blocks.dtype)
    blocks[1, count] = jnp.zeros(blocks.shape[2:], blocks.dtype)

    load_dims.wait()
    load_raw.wait()
    columns = lax.broadcasted_iota(jnp.int32, raw.shape, 1)
    masked = jnp.where(columns < dims[0], raw[...].astype(jnp.float32), 0.0)
    mine[...] = masked.astype(jnp.bfloat16)
    own_rows = gap.shape[0]
    for group in range(pairs):
        mine_wide[group] = masked[group * own_rows : (group + 1) * own_rows]
    major = jnp.where(kind == 0, y, z)
    minor = jnp.where(kind == 0, z, y) // 2
    slot = gathered.at[kind, major, minor]
    keep = pltpu.make_async_copy(mine, slot, first_recv.at[kind, minor // GROUP])
    keep.start()

    pl.semaphore_wait(barrier, 2 * (RING - 1) + 2 * (pairs - 1) + 1)

    first = []
    for step in STEPS:
        copy = pltpu.make_async_remote_copy(
            src_ref=mine,
            dst_ref=slot,
            send_sem=first_send.at[step - 1],
            recv_sem=first_recv.at[kind, minor // GROUP],
            device_id={"tiles": jnp.where(kind == 0, along_z(step), along_y(step))},
        )
        copy.start()
        first.append(copy)

    partner_copies = []
    for i in range(CHUNKS):
        rows = pl.ds(i * part, part)
        copy = pltpu.make_async_remote_copy(
            src_ref=integrals.at[0, 0, rows],
            dst_ref=blocks.at[1, rows],
            send_sem=partner_send.at[i],
            recv_sem=partner_recv.at[i],
            device_id={"tiles": partner},
        )
        copy.start()
        partner_copies.append(copy)

    load_owners.wait()
    width = raw.shape[1]
    row = jnp.broadcast_to(owners[...], (width, count))
    row = jnp.concatenate([row, jnp.full((width, width - count), -1, jnp.int32)], axis=1)
    named = row.T == lax.broadcasted_iota(jnp.int32, (width, width), 1)
    places = lax.broadcasted_iota(jnp.int32, (width, width), 0)
    place = jnp.min(jnp.where(named, places, count), axis=0, keepdims=True)
    entry_rows[0] = jnp.broadcast_to(place, entry_rows.shape[1:])
    copy = pltpu.make_async_remote_copy(
        src_ref=entry_rows.at[0],
        dst_ref=entry_rows.at[1],
        send_sem=partner_send.at[CHUNKS],
        recv_sem=partner_recv.at[CHUNKS],
        device_id={"tiles": partner},
    )
    copy.start()
    partner_copies.append(copy)
    own_entries = pltpu.make_async_copy(entry_rows.at[0], entries.at[0], entry_sems.at[0])
    own_entries.start()

    second = {}
    for group in range(GROUPS):
        for which in range(2):
            ref = gathered.at[which, 0, pl.ds(0, GROUP)]
            pltpu.make_async_copy(ref, ref, first_recv.at[which, group]).wait()
        for step in STEPS:
            for which in range(2):
                line = y if which == 0 else z
                ref = gathered.at[which, line, pl.ds(group * GROUP, GROUP)]
                copy = pltpu.make_async_remote_copy(
                    src_ref=ref,
                    dst_ref=ref,
                    send_sem=second_send.at[which, group, step - 1],
                    recv_sem=second_recv.at[which, group, step - 1],
                    device_id={"tiles": along_y(step) if which == 0 else along_z(step)},
                )
                copy.start()
                second[which, group, step] = copy

    for load in load_blocks:
        load.wait()
    partner_copies[CHUNKS].wait_recv()
    their_entries = pltpu.make_async_copy(entry_rows.at[1], entries.at[1], entry_sems.at[1])
    their_entries.start()
    for copy in partner_copies[:CHUNKS]:
        copy.wait_recv()
    own_entries.wait()
    their_entries.wait()

    def product(which, line, index):
        low = 2 * index + (line + which) % 2
        source = (line * RING + low if which == 0 else low * RING + line) * 2 + core
        listed = [blocks[which_list, entries[which_list, 0, source]] for which_list in range(2)]
        return gathered[which, line, index], jnp.concatenate(listed, axis=0)

    total = jnp.zeros((raw.shape[0], 2 * width), jnp.float32)

    def add_line(total, which, line, group):
        pieces = [product(which, line, group * GROUP + i) for i in range(GROUP)]
        left = jnp.concatenate([piece[0] for piece in pieces], axis=1)
        right = jnp.concatenate([piece[1] for piece in pieces], axis=1)
        return total + lax.dot_general(left, right, NT_DIMS, preferred_element_type=jnp.float32)

    for group in range(GROUPS):
        for which in range(2):
            total = add_line(total, which, y if which == 0 else z, group)
        for step in reversed(STEPS):
            for which in range(2):
                second[which, group, step].wait_recv()
                line = ((y if which == 0 else z) + RING - step) % RING
                total = add_line(total, which, line, group)
    for which_list in range(2):
        for group in range(pairs):
            terms[which_list, group] = total[
                group * own_rows : (group + 1) * own_rows,
                which_list * width : (which_list + 1) * width,
            ]

    sums = []
    for step in (2, 1, 3, 0):
        other = (pair + step) % pairs
        for which_list in (1, 0):
            if step == 0 and which_list == 0:
                continue
            number = which_list * pairs + step - 1
            copy = pltpu.make_async_remote_copy(
                src_ref=terms.at[which_list, other],
                dst_ref=arrived.at[number],
                send_sem=sum_send.at[number],
                recv_sem=sum_recv.at[number],
                device_id={"tiles": partner if which_list else tile, "pairs": other},
            )
            copy.start()
            sums.append(copy)
    load_gap.wait()
    keep_sends = first + list(second.values()) + partner_copies
    for copy in keep_sends:
        copy.wait_send()
    for copy in sums:
        copy.wait_recv()
    summed = terms[0, pair]
    for number in range(2 * pairs - 1):
        summed += arrived[number]
    live = lax.broadcasted_iota(jnp.int32, summed.shape, 1) < dims[0]
    summed = jnp.where(live, summed, 0.0)
    out[:own_rows] = summed
    out[own_rows:] = mine_wide[pair] - summed / gap[...]
    for copy in sums:
        copy.wait_send()


def per_device(amplitudes, integrals, block_owner, tile_dims, energy_gap):
    rows, width = amplitudes.shape
    count = integrals.shape[2]
    own_rows = energy_gap.shape[0]
    pairs = rows // own_rows
    dma = pltpu.SemaphoreType.DMA
    out = pl.pallas_call(
        kernel,
        out_shape=jax.ShapeDtypeStruct((2 * own_rows, width), jnp.float32),
        in_specs=[pl.BlockSpec(memory_space=pltpu.HBM)] * 5,
        out_specs=pl.BlockSpec(memory_space=pltpu.VMEM),
        scratch_shapes=[
            pltpu.VMEM((1, count), jnp.int32),
            pltpu.SMEM((1,), jnp.int32),
            pltpu.VMEM((rows, width), jnp.bfloat16),
            pltpu.VMEM((own_rows, width), jnp.float32),
            pltpu.VMEM((2, count + 1, width, width), jnp.bfloat16),
            pltpu.VMEM((rows, width), jnp.bfloat16),
            pltpu.VMEM((pairs, own_rows, width), jnp.float32),
            pltpu.VMEM((2, RING, HALF, rows, width), jnp.bfloat16),
            pltpu.VMEM((2, 8, width), jnp.int32),
            pltpu.SMEM((2, 8, width), jnp.int32),
            pltpu.VMEM((2, pairs, own_rows, width), jnp.float32),
            pltpu.VMEM((2 * pairs - 1, own_rows, width), jnp.float32),
            dma((4 + CHUNKS,)),
            dma((2,)),
            dma((CHUNKS + 1,)),
            dma((CHUNKS + 1,)),
            dma((RING - 1,)),
            dma((2, GROUPS)),
            dma((2, GROUPS, RING - 1)),
            dma((2, GROUPS, RING - 1)),
            dma((2 * pairs - 1,)),
            dma((2 * pairs - 1,)),
        ],
        compiler_params=pltpu.CompilerParams(
            collective_id=0, has_side_effects=True, vmem_limit_bytes=62 * 2**20
        ),
        cost_estimate=pl.CostEstimate(
            flops=2 * count * rows * width * width,
            bytes_accessed=2 * count * width * width,
            transcendentals=0,
        ),
    )(block_owner.reshape(1, count), tile_dims, amplitudes, integrals, energy_gap)
    return out[:own_rows], out[own_rows:].astype(jnp.bfloat16)


def solution(mesh):
    in_specs = (
        P(None, "tiles"),
        P("tiles", "pairs", None, None, None),
        P("tiles", "pairs", None, None),
        P("tiles"),
        P("pairs", "tiles"),
    )
    out_specs = (P("pairs", "tiles"), P("pairs", "tiles"))
    return jax.shard_map(
        per_device, mesh=mesh, in_specs=in_specs, out_specs=out_specs, check_vma=False
    )
```

time: 214 us -> 35.9 us (0.17)
  the two profiles are of different devices: /device:TPU:8 before, /device:TPU:1 now
where the time goes in v1:
time: 35.9 us; the launch traced here: 35.7 us
  Pallas kernels  31.9 us (89%)
  local copies, waits for them, and re-layouts  2.54 us (7%)
  between operations  1.29 us (4%)
    pallas_call x1, Pallas kernels, per_device(): pl.pallas_call(kernel, out_shape=jax.ShapeDtypeStruct((2 * own_rows, widt...  31.9 us
    slice x2, local copies, waits for them, and re-layouts, per_device(): return (out[:own_rows], out[own_rows:].astype(jnp.bfloat16))  2.54 us

profile of v1, /device:TPU:1, one launch (start us, length us, event | category | flops | bytes accessed | tf_op | source)
XLA Modules:
  0.0 35.7 jit_solution(6487504755147382648)
XLA Ops:
  1.3 31.9 %shard_map.68 = f32[16,128]{1,0:T(8,128)} custom-call(s32[1,96]{1,0:T(1,128)} %bitcast.1, s32[1]{0:T(128)S(6)} %copy.7.dims_in, bf16[32,128]{1,0:T(8,128)(2,1)} %amplitudes.1, bf16[1,1,96,128,128]{4,3,2,1,0:T(8,128)(2,1)} %integrals.1, f32[8,128]{1,0:T(8,128)} %energy_gap.1), custom_call_target="tpu_custom_call" | custom-call | flops 100663296 | bytes 3145728 | tf_op jit(solution)/shard_map/pallas_call | solution.py:252
  33.1 1.3 %slice.11 = bf16[8,128]{1,0:T(8,128)(2,1)} slice(f32[16,128]{1,0:T(8,128)} %shard_map.68), slice={[8:16], [0:128]} | slice | bytes 4096 | tf_op jit(solution)/shard_map/slice | solution.py:290
  34.4 1.3 %slice.7 = f32[8,128]{1,0:T(8,128)} slice(f32[16,128]{1,0:T(8,128)} %shard_map.68), slice={[0:8], [0:128]} | slice | bytes 8192 | tf_op jit(solution)/shard_map/slice | solution.py:290

commit v2 on v1

--- a/solution.py
+++ b/solution.py
@@ -11,6 +11,7 @@
 GROUPS = HALF // GROUP
 CHUNKS = 4
 STEPS = (4, 3, 5, 2, 6, 1, 7)
+EARLY, LATE = range(HALF), range(HALF, RING)
 NT_DIMS = (((1,), (1,)), ((), ()))
 
 
@@ -19,12 +20,10 @@
     dims_in,
     amplitudes,
     integrals,
-    energy_gap,
     out,
     owners,
     dims,
     raw,
-    gap,
     blocks,
     mine,
     mine_wide,
@@ -37,9 +36,13 @@
     entry_sems,
     partner_send,
     partner_recv,
-    first_send,
+    late_in,
+    late_go,
+    row_send,
+    column_send,
     first_recv,
-    second_send,
+    row_line_send,
+    column_line_send,
     second_recv,
     sum_send,
     sum_recv,
@@ -55,8 +58,10 @@
     count = blocks.shape[1] - 1
     part = count // CHUNKS
 
-    def along_z(step):
-        return (y * RING + (z + step) % RING) * 2 + core
+    early = z < HALF
+
+    def in_row(column):
+        return (y * RING + column) * 2 + core
 
     def along_y(step):
         return (((y + step) % RING) * RING + z) * 2 + core
@@ -64,13 +69,11 @@
     load_raw = pltpu.make_async_copy(amplitudes, raw, load_sems.at[0])
     load_dims = pltpu.make_async_copy(dims_in, dims, load_sems.at[1])
     load_owners = pltpu.make_async_copy(owners_in, owners, load_sems.at[2])
-    load_gap = pltpu.make_async_copy(energy_gap, gap, load_sems.at[3])
     load_raw.start()
     load_dims.start()
 
     barrier = pltpu.get_barrier_semaphore()
     for step in STEPS:
-        pl.semaphore_signal(barrier, inc=1, device_id={"tiles": along_z(step)})
         pl.semaphore_signal(barrier, inc=1, device_id={"tiles": along_y(step)})
     for step in range(1, pairs):
         other = (pair + step) % pairs
@@ -78,13 +81,17 @@
         pl.semaphore_signal(barrier, inc=1, device_id={"tiles": partner, "pairs": other})
     pl.semaphore_signal(barrier, inc=1, device_id={"tiles": partner})
 
+    @pl.when(early)
+    def _():
+        for step in STEPS:
+            pl.semaphore_signal(barrier, inc=1, device_id={"tiles": in_row((z + step) % RING)})
+
     load_owners.start()
-    load_gap.start()
     load_blocks = []
     for i in range(CHUNKS):
         rows = pl.ds(i * part, part)
         load = pltpu.make_async_copy(
-            integrals.at[0, 0, rows], blocks.at[0, rows], load_sems.at[4 + i]
+            integrals.at[0, 0, rows], blocks.at[0, rows], load_sems.at[3 + i]
         )
         load.start()
         load_blocks.append(load)
@@ -96,7 +103,7 @@
     columns = lax.broadcasted_iota(jnp.int32, raw.shape, 1)
     masked = jnp.where(columns < dims[0], raw[...].astype(jnp.float32), 0.0)
     mine[...] = masked.astype(jnp.bfloat16)
-    own_rows = gap.shape[0]
+    own_rows = terms.shape[2]
     for group in range(pairs):
         mine_wide[group] = masked[group * own_rows : (group + 1) * own_rows]
     major = jnp.where(kind == 0, y, z)
@@ -105,19 +112,41 @@
     keep = pltpu.make_async_copy(mine, slot, first_recv.at[kind, minor // GROUP])
     keep.start()
 
-    pl.semaphore_wait(barrier, 2 * (RING - 1) + 2 * (pairs - 1) + 1)
-
-    first = []
+    from_row = jnp.where(early, HALF - 1, HALF)
+    pl.semaphore_wait(barrier, RING - 1 + 2 * (pairs - 1) + 1 + from_row)
+
+    row_copies = []
+    for column in range(RING):
+        copy = pltpu.make_async_remote_copy(
+            src_ref=mine,
+            dst_ref=slot,
+            send_sem=row_send.at[column],
+            recv_sem=first_recv.at[0, minor // GROUP],
+            device_id={"tiles": in_row(column)},
+        )
+        row_copies.append((jnp.logical_and(kind == 0, z != column), copy))
+    column_copies = []
     for step in STEPS:
         copy = pltpu.make_async_remote_copy(
             src_ref=mine,
             dst_ref=slot,
-            send_sem=first_send.at[step - 1],
-            recv_sem=first_recv.at[kind, minor // GROUP],
-            device_id={"tiles": jnp.where(kind == 0, along_z(step), along_y(step))},
+            send_sem=column_send.at[step - 1],
+            recv_sem=first_recv.at[1, minor // GROUP],
+            device_id={"tiles": along_y(step)},
         )
-        copy.start()
-        first.append(copy)
+        column_copies.append((kind == 1, copy))
+    for column in EARLY:
+        pl.when(row_copies[column][0])(row_copies[column][1].start)
+
+    @pl.when(kind == 1)
+    def _():
+        for _, copy in column_copies:
+            copy.start()
+
+    @pl.when(jnp.logical_not(early))
+    def _():
+        for column in EARLY:
+            pl.semaphore_signal(late_in, inc=1, device_id={"tiles": in_row(column)})
 
     partner_copies = []
     for i in range(CHUNKS):
@@ -152,24 +181,62 @@
     own_entries = pltpu.make_async_copy(entry_rows.at[0], entries.at[0], entry_sems.at[0])
     own_entries.start()
 
-    second = {}
+    def wait_first(which, group):
+        ref = gathered.at[which, 0, pl.ds(0, GROUP)]
+        pltpu.make_async_copy(ref, ref, first_recv.at[which, group]).wait()
+
+    row_lines = {}
     for group in range(GROUPS):
-        for which in range(2):
-            ref = gathered.at[which, 0, pl.ds(0, GROUP)]
-            pltpu.make_async_copy(ref, ref, first_recv.at[which, group]).wait()
+        for column in range(RING):
+            ref = gathered.at[1, z, pl.ds(group * GROUP, GROUP)]
+            copy = pltpu.make_async_remote_copy(
+                src_ref=ref,
+                dst_ref=ref,
+                send_sem=row_line_send.at[group, column],
+                recv_sem=second_recv.at[1, group, (column + RING - 1 - z) % RING],
+                device_id={"tiles": in_row(column)},
+            )
+            row_lines[group, column] = (z != column, copy)
+    def send_early_lines():
+        for group in range(GROUPS):
+            wait_first(1, group)
+            for column in EARLY:
+                pl.when(row_lines[group, column][0])(row_lines[group, column][1].start)
+
+    @pl.when(early)
+    def _():
+        send_early_lines()
+        pl.semaphore_wait(late_in, HALF)
+
+    @pl.when(z == 0)
+    def _():
+        for column in LATE:
+            pl.semaphore_signal(late_go, inc=1, device_id={"tiles": in_row(column)})
+
+    @pl.when(jnp.logical_not(early))
+    def _():
+        send_early_lines()
+        pl.semaphore_wait(late_go, 1)
+
+    for column in LATE:
+        pl.when(row_copies[column][0])(row_copies[column][1].start)
+    for group in range(GROUPS):
+        for column in LATE:
+            pl.when(row_lines[group, column][0])(row_lines[group, column][1].start)
+    column_lines = {}
+    for group in range(GROUPS):
+        wait_first(0, group)
         for step in STEPS:
-            for which in range(2):
-                line = y if which == 0 else z
-                ref = gathered.at[which, line, pl.ds(group * GROUP, GROUP)]
-                copy = pltpu.make_async_remote_copy(
-                    src_ref=ref,
-                    dst_ref=ref,
-                    send_sem=second_send.at[which, group, step - 1],
-                    recv_sem=second_recv.at[which, group, step - 1],
-                    device_id={"tiles": along_y(step) if which == 0 else along_z(step)},
-                )
-                copy.start()
-                second[which, group, step] = copy
+            ref = gathered.at[0, y, pl.ds(group * GROUP, GROUP)]
+            copy = pltpu.make_async_remote_copy(
+                src_ref=ref,
+                dst_ref=ref,
+                send_sem=column_line_send.at[group, step - 1],
+                recv_sem=second_recv.at[0, group, step - 1],
+                device_id={"tiles": along_y(step)},
+            )
+            copy.start()
+            column_lines[group, step] = copy
 
     for load in load_blocks:
         load.wait()
@@ -200,7 +267,8 @@
             total = add_line(total, which, y if which == 0 else z, group)
         for step in reversed(STEPS):
             for which in range(2):
-                second[which, group, step].wait_recv()
+                ref = gathered.at[which, 0, pl.ds(0, GROUP)]
+                pltpu.make_async_copy(ref, ref, second_recv.at[which, group, step - 1]).wait()
                 line = ((y if which == 0 else z) + RING - step) % RING
                 total = add_line(total, which, line, group)
     for which_list in range(2):
@@ -226,19 +294,22 @@
             )
             copy.start()
             sums.append(copy)
-    load_gap.wait()
-    keep_sends = first + list(second.values()) + partner_copies
-    for copy in keep_sends:
+    for copy in partner_copies + list(column_lines.values()):
         copy.wait_send()
+    for sent, copy in row_copies + column_copies + list(row_lines.values()):
+        pl.when(sent)(copy.wait_send)
     for copy in sums:
         copy.wait_recv()
-    summed = terms[0, pair]
-    for number in range(2 * pairs - 1):
-        summed += arrived[number]
-    live = lax.broadcasted_iota(jnp.int32, summed.shape, 1) < dims[0]
-    summed = jnp.where(live, summed, 0.0)
-    out[:own_rows] = summed
-    out[own_rows:] = mine_wide[pair] - summed / gap[...]
+    near = terms[0, pair]
+    for number in range(pairs - 1):
+        near += arrived[number]
+    far = arrived[pairs - 1]
+    for number in range(pairs, 2 * pairs - 1):
+        far += arrived[number]
+    live = lax.broadcasted_iota(jnp.int32, near.shape, 1) < dims[0]
+    out[0] = jnp.where(live, near, 0.0)
+    out[1] = jnp.where(live, far, 0.0)
+    out[2] = mine_wide[pair]
     for copy in sums:
         copy.wait_send()
 
@@ -251,14 +322,13 @@
     dma = pltpu.SemaphoreType.DMA
     out = pl.pallas_call(
         kernel,
-        out_shape=jax.ShapeDtypeStruct((2 * own_rows, width), jnp.float32),
-        in_specs=[pl.BlockSpec(memory_space=pltpu.HBM)] * 5,
+        out_shape=jax.ShapeDtypeStruct((3, own_rows, width), jnp.float32),
+        in_specs=[pl.BlockSpec(memory_space=pltpu.HBM)] * 4,
         out_specs=pl.BlockSpec(memory_space=pltpu.VMEM),
         scratch_shapes=[
             pltpu.VMEM((1, count), jnp.int32),
             pltpu.SMEM((1,), jnp.int32),
             pltpu.VMEM((rows, width), jnp.bfloat16),
-            pltpu.VMEM((own_rows, width), jnp.float32),
             pltpu.VMEM((2, count + 1, width, width), jnp.bfloat16),
             pltpu.VMEM((rows, width), jnp.bfloat16),
             pltpu.VMEM((pairs, own_rows, width), jnp.float32),
@@ -267,14 +337,18 @@
             pltpu.SMEM((2, 8, width), jnp.int32),
             pltpu.VMEM((2, pairs, own_rows, width), jnp.float32),
             pltpu.VMEM((2 * pairs - 1, own_rows, width), jnp.float32),
-            dma((4 + CHUNKS,)),
+            dma((3 + CHUNKS,)),
             dma((2,)),
             dma((CHUNKS + 1,)),
             dma((CHUNKS + 1,)),
+            pltpu.SemaphoreType.REGULAR,
+            pltpu.SemaphoreType.REGULAR,
+            dma((RING,)),
             dma((RING - 1,)),
             dma((2, GROUPS)),
-            dma((2, GROUPS, RING - 1)),
-            dma((2, GROUPS, RING - 1)),
+            dma((GROUPS, RING)),
+            dma((GROUPS, RING - 1)),
+            dma((2, GROUPS, RING)),
             dma((2 * pairs - 1,)),
             dma((2 * pairs - 1,)),
         ],
@@ -286,8 +360,9 @@
             bytes_accessed=2 * count * width * width,
             transcendentals=0,
         ),
-    )(block_owner.reshape(1, count), tile_dims, amplitudes, integrals, energy_gap)
-    return out[:own_rows], out[own_rows:].astype(jnp.bfloat16)
+    )(block_owner.reshape(1, count), tile_dims, amplitudes, integrals)
+    residual = out[0] + out[1]
+    return residual, (out[2] - residual / energy_gap).astype(jnp.bfloat16)
 
 
 def solution(mesh):

time: 35.9 us -> 33.7 us (0.939)
  local copies, waits for them, and re-layouts: 2.54 us -> 0.01 us
  other arithmetic: 0 us -> 1.29 us
  Pallas kernels: 31.9 us -> 30.9 us
    slice x2 -> x0, local copies, waits for them, and re-layouts: 2.54 us -> none  [per_device(): return (out[:own_rows], out[own_rows:].astype(jnp.bfloat16))]
    convert_element_type x0 -> x1, other arithmetic: none -> 1.29 us  [per_device(): return (residual, (out[2] - residual / energy_gap).astype(jnp.bfloat16))]
    pallas_call x1, Pallas kernels: 31.9 us -> 30.9 us  [per_device(): pl.pallas_call(kernel, out_shape=jax.ShapeDtypeStruct((3, own_rows, width...]
where the time goes in v2:
time: 33.7 us; the launch traced here: 33.5 us
  Pallas kernels  30.9 us (92%)
  between operations  1.31 us (4%)
  other arithmetic  1.29 us (4%)
    pallas_call x1, Pallas kernels, per_device(): pl.pallas_call(kernel, out_shape=jax.ShapeDtypeStruct((3, own_rows, width...  30.9 us
    convert_element_type x1, other arithmetic, per_device(): return (residual, (out[2] - residual / energy_gap).astype(jnp.bfloat16))  1.29 us

profile of v2, /device:TPU:1, one launch (start us, length us, event | category | flops | bytes accessed | tf_op | source)
XLA Modules:
  0.0 33.5 jit_solution(9314769378438014807)
XLA Ops:
  0.6 0.0 copy-start
  1.3 30.9 %shard_map.68 = f32[3,8,128]{2,1,0:T(8,128)} custom-call(s32[1,96]{1,0:T(1,128)} %bitcast.8, s32[1]{0:T(128)S(6)} %copy.7.dims_in, bf16[32,128]{1,0:T(8,128)(2,1)} %amplitudes.1, bf16[1,1,96,128,128]{4,3,2,1,0:T(8,128)(2,1)} %integrals.1), custom_call_target="tpu_custom_call" | custom-call | flops 100663296 | bytes 3145728 | tf_op jit(solution)/shard_map/pallas_call | solution.py:323
  32.2 0.0 copy-done
  32.2 1.3 %fusion = (bf16[8,128]{1,0:T(8,128)(2,1)}, f32[8,128]{1,0:T(8,128)}) fusion(f32[8,128]{1,0:T(8,128)S(1)} %copy-done, f32[3,8,128]{2,1,0:T(8,128)} %shard_map.68), kind=kLoop, calls=%fused_computation.1 | loop fusion | flops 4096 | bytes 22528 | tf_op jit(solution)/shard_map/convert_element_type | solution.py:365
Async XLA Ops:
  0.6 31.6 %copy-start = (f32[8,128]{1,0:T(8,128)S(1)}, f32[8,128]{1,0:T(8,128)}, u32[]{:S(2)}) copy-start(f32[8,128]{1,0:T(8,128)} %param.9) | copy-start | bytes 12292

commit v3 on v2

--- a/solution.py
+++ b/solution.py
@@ -11,6 +11,7 @@
 GROUPS = HALF // GROUP
 CHUNKS = 4
 STEPS = (4, 3, 5, 2, 6, 1, 7)
+ROWS = (0, 1, 2, 3, 7, 6, 5, 4)
 EARLY, LATE = range(HALF), range(HALF, RING)
 NT_DIMS = (((1,), (1,)), ((), ()))
 
@@ -36,6 +37,9 @@
     entry_sems,
     partner_send,
     partner_recv,
+    straight_send,
+    row_in,
+    column_in,
     late_in,
     late_go,
     row_send,
@@ -73,8 +77,14 @@
     load_dims.start()
 
     barrier = pltpu.get_barrier_semaphore()
-    for step in STEPS:
-        pl.semaphore_signal(barrier, inc=1, device_id={"tiles": along_y(step)})
+    for which in range(2):
+
+        @pl.when(kind == which)
+        def _():
+            for step in STEPS:
+                if (which + step) % 2 == 1:
+                    pl.semaphore_signal(barrier, inc=1, device_id={"tiles": along_y(step)})
+
     for step in range(1, pairs):
         other = (pair + step) % pairs
         pl.semaphore_signal(barrier, inc=1, device_id={"pairs": other})
@@ -83,8 +93,31 @@
 
     @pl.when(early)
     def _():
-        for step in STEPS:
-            pl.semaphore_signal(barrier, inc=1, device_id={"tiles": in_row((z + step) % RING)})
+        for column in LATE:
+            pl.semaphore_signal(barrier, inc=1, device_id={"tiles": in_row(column)})
+        for column in EARLY:
+
+            @pl.when(jnp.logical_and(z != column, (y + column) % 2 == 0))
+            def _():
+                pl.semaphore_signal(barrier, inc=1, device_id={"tiles": in_row(column)})
+
+    mate = in_row(z + 1 - 2 * (z % 2))
+
+    @pl.when(jnp.logical_and(kind == 1, jnp.logical_not(early)))
+    def _():
+        pl.semaphore_signal(barrier, inc=1, device_id={"tiles": mate})
+
+    @pl.when(z == 0)
+    def _():
+        for step in range(RING):
+            for column in range(1, RING):
+                if step == 0 and column >= HALF:
+                    continue
+                other = (((y + step) % RING) * RING + column) * 2 + core
+
+                @pl.when((y + step + column) % 2 == 1)
+                def _():
+                    pl.semaphore_signal(barrier, inc=1, device_id={"tiles": other})
 
     load_owners.start()
     load_blocks = []
@@ -112,8 +145,27 @@
     keep = pltpu.make_async_copy(mine, slot, first_recv.at[kind, minor // GROUP])
     keep.start()
 
-    from_row = jnp.where(early, HALF - 1, HALF)
-    pl.semaphore_wait(barrier, RING - 1 + 2 * (pairs - 1) + 1 + from_row)
+    from_row = jnp.where(early, jnp.where(kind == 0, HALF - 1, 0), HALF + 1 - kind)
+    from_column = jnp.where(kind == 0, 0, RING - 1)
+    straight = jnp.logical_and(kind == 1, z != 0)
+    from_first = jnp.where(straight, jnp.where(early, RING, RING - 1), 0)
+    pl.semaphore_wait(barrier, 2 * (pairs - 1) + 1 + from_row + from_column + from_first)
+
+    straight_copies = [
+        pltpu.make_async_remote_copy(
+            src_ref=mine,
+            dst_ref=slot,
+            send_sem=straight_send.at[row],
+            recv_sem=second_recv.at[1, minor // GROUP, RING - 1 - z],
+            device_id={"tiles": row * RING * 2 + core},
+        )
+        for row in ROWS
+    ]
+
+    @pl.when(straight)
+    def _():
+        for copy in straight_copies:
+            copy.start()
 
     row_copies = []
     for column in range(RING):
@@ -140,10 +192,15 @@
 
     @pl.when(kind == 1)
     def _():
+        pl.semaphore_signal(column_in, inc=1, device_id={"tiles": along_y(1)})
         for _, copy in column_copies:
             copy.start()
 
-    @pl.when(jnp.logical_not(early))
+    @pl.when(jnp.logical_and(kind == 0, early))
+    def _():
+        pl.semaphore_signal(row_in, inc=1, device_id={"tiles": mate})
+
+    @pl.when(jnp.logical_and(kind == 0, jnp.logical_not(early)))
     def _():
         for column in EARLY:
             pl.semaphore_signal(late_in, inc=1, device_id={"tiles": in_row(column)})
@@ -187,7 +244,7 @@
 
     row_lines = {}
     for group in range(GROUPS):
-        for column in range(RING):
+        for column in range(1, RING):
             ref = gathered.at[1, z, pl.ds(group * GROUP, GROUP)]
             copy = pltpu.make_async_remote_copy(
                 src_ref=ref,
@@ -197,47 +254,71 @@
                 device_id={"tiles": in_row(column)},
             )
             row_lines[group, column] = (z != column, copy)
-    def send_early_lines():
-        for group in range(GROUPS):
-            wait_first(1, group)
-            for column in EARLY:
-                pl.when(row_lines[group, column][0])(row_lines[group, column][1].start)
-
-    @pl.when(early)
-    def _():
-        send_early_lines()
-        pl.semaphore_wait(late_in, HALF)
-
-    @pl.when(z == 0)
-    def _():
-        for column in LATE:
-            pl.semaphore_signal(late_go, inc=1, device_id={"tiles": in_row(column)})
-
-    @pl.when(jnp.logical_not(early))
-    def _():
-        send_early_lines()
-        pl.semaphore_wait(late_go, 1)
-
-    for column in LATE:
-        pl.when(row_copies[column][0])(row_copies[column][1].start)
-    for group in range(GROUPS):
-        for column in LATE:
-            pl.when(row_lines[group, column][0])(row_lines[group, column][1].start)
     column_lines = {}
     for group in range(GROUPS):
-        wait_first(0, group)
-        for step in STEPS:
+        for row in ROWS:
             ref = gathered.at[0, y, pl.ds(group * GROUP, GROUP)]
             copy = pltpu.make_async_remote_copy(
                 src_ref=ref,
                 dst_ref=ref,
-                send_sem=column_line_send.at[group, step - 1],
-                recv_sem=second_recv.at[0, group, step - 1],
-                device_id={"tiles": along_y(step)},
+                send_sem=column_line_send.at[group, row],
+                recv_sem=second_recv.at[0, group, (row + RING - 1 - y) % RING],
+                device_id={"tiles": (row * RING + z) * 2 + core},
             )
-            copy.start()
-            column_lines[group, step] = copy
-
+            column_lines[group, row] = (y != row, copy)
+
+    def send_column_lines(groups):
+        for group in groups:
+            wait_first(0, group)
+            for row in ROWS:
+                pl.when(column_lines[group, row][0])(column_lines[group, row][1].start)
+
+    def send_early_lines():
+        for group in range(GROUPS):
+            wait_first(1, group)
+            for column in EARLY[1:]:
+                pl.when(row_lines[group, column][0])(row_lines[group, column][1].start)
+
+    @pl.when(early)
+    def _():
+        @pl.when(kind == 1)
+        def _():
+            pl.semaphore_wait(row_in, 1)
+
+        send_early_lines()
+
+        @pl.when(kind == 0)
+        def _():
+            pl.semaphore_wait(column_in, 1)
+
+        send_column_lines(range(GROUPS // 2))
+        pl.semaphore_wait(late_in, HALF // 2)
+
+    @pl.when(z == 0)
+    def _():
+        for column in LATE:
+            pl.semaphore_signal(late_go, inc=1, device_id={"tiles": in_row(column)})
+
+    @pl.when(jnp.logical_not(early))
+    def _():
+        pl.semaphore_wait(late_go, 1)
+
+    for column in (6, 5, 7, 4):
+        pl.when(row_copies[column][0])(row_copies[column][1].start)
+    pl.when(jnp.logical_not(early))(send_early_lines)
+    @pl.when(jnp.logical_not(early))
+    def _():
+        @pl.when(kind == 0)
+        def _():
+            pl.semaphore_wait(column_in, 1)
+
+        send_column_lines(range(GROUPS // 2))
+
+    send_column_lines(range(GROUPS // 2, GROUPS))
+
+    for group in range(GROUPS):
+        for column in (6, 5, 7, 4):
+            pl.when(row_lines[group, column][0])(row_lines[group, column][1].start)
     for load in load_blocks:
         load.wait()
     partner_copies[CHUNKS].wait_recv()
@@ -294,10 +375,17 @@
             )
             copy.start()
             sums.append(copy)
-    for copy in partner_copies + list(column_lines.values()):
+    for copy in partner_copies:
         copy.wait_send()
-    for sent, copy in row_copies + column_copies + list(row_lines.values()):
+    lines = list(row_lines.values()) + list(column_lines.values())
+    for sent, copy in row_copies + column_copies + lines:
         pl.when(sent)(copy.wait_send)
+
+    @pl.when(straight)
+    def _():
+        for copy in straight_copies:
+            copy.wait_send()
+
     for copy in sums:
         copy.wait_recv()
     near = terms[0, pair]
@@ -341,13 +429,16 @@
             dma((2,)),
             dma((CHUNKS + 1,)),
             dma((CHUNKS + 1,)),
+            dma((RING,)),
+            pltpu.SemaphoreType.REGULAR,
+            pltpu.SemaphoreType.REGULAR,
             pltpu.SemaphoreType.REGULAR,
             pltpu.SemaphoreType.REGULAR,
             dma((RING,)),
             dma((RING - 1,)),
             dma((2, GROUPS)),
             dma((GROUPS, RING)),
-            dma((GROUPS, RING - 1)),
+            dma((GROUPS, RING)),
             dma((2, GROUPS, RING)),
             dma((2 * pairs - 1,)),
             dma((2 * pairs - 1,)),

time: 33.7 us -> 32 us (0.950)
  Pallas kernels: 30.9 us -> 29.2 us
    pallas_call x1, Pallas kernels: 30.9 us -> 29.2 us  [per_device(): pl.pallas_call(kernel, out_shape=jax.ShapeDtypeStruct((3, own_rows, width...]
where the time goes in v3:
time: 32 us; the launch traced here: 31.8 us
  Pallas kernels  29.2 us (91%)
  between operations  1.31 us (4%)
  other arithmetic  1.29 us (4%)
    pallas_call x1, Pallas kernels, per_device(): pl.pallas_call(kernel, out_shape=jax.ShapeDtypeStruct((3, own_rows, width...  29.2 us
    convert_element_type x1, other arithmetic, per_device(): return (residual, (out[2] - residual / energy_gap).astype(jnp.bfloat16))  1.29 us

profile of v3, /device:TPU:1, one launch (start us, length us, event | category | flops | bytes accessed | tf_op | source)
XLA Modules:
  0.0 31.8 jit_solution(4021186348537724616)
XLA Ops:
  0.6 0.0 copy-start
  1.3 29.2 %shard_map.68 = f32[3,8,128]{2,1,0:T(8,128)} custom-call(s32[1,96]{1,0:T(1,128)} %bitcast.8, s32[1]{0:T(128)S(6)} %copy.7.dims_in, bf16[32,128]{1,0:T(8,128)(2,1)} %amplitudes.1, bf16[1,1,96,128,128]{4,3,2,1,0:T(8,128)(2,1)} %integrals.1), custom_call_target="tpu_custom_call" | custom-call | flops 100663296 | bytes 3145728 | tf_op jit(solution)/shard_map/pallas_call | solution.py:411
  30.5 0.0 copy-done
  30.5 1.3 %fusion = (bf16[8,128]{1,0:T(8,128)(2,1)}, f32[8,128]{1,0:T(8,128)}) fusion(f32[8,128]{1,0:T(8,128)S(1)} %copy-done, f32[3,8,128]{2,1,0:T(8,128)} %shard_map.68), kind=kLoop, calls=%fused_computation.1 | loop fusion | flops 4096 | bytes 22528 | tf_op jit(solution)/shard_map/convert_element_type | solution.py:456
Async XLA Ops:
  0.6 29.9 %copy-start = (f32[8,128]{1,0:T(8,128)S(1)}, f32[8,128]{1,0:T(8,128)}, u32[]{:S(2)}) copy-start(f32[8,128]{1,0:T(8,128)} %param.9) | copy-start | bytes 12292

commit v4 on v3

--- a/solution.py
+++ b/solution.py
@@ -281,17 +281,17 @@
 
     @pl.when(early)
     def _():
+        @pl.when(kind == 0)
+        def _():
+            pl.semaphore_wait(column_in, 1)
+
+        send_column_lines(range(GROUPS // 2))
+
         @pl.when(kind == 1)
         def _():
             pl.semaphore_wait(row_in, 1)
 
         send_early_lines()
-
-        @pl.when(kind == 0)
-        def _():
-            pl.semaphore_wait(column_in, 1)
-
-        send_column_lines(range(GROUPS // 2))
         pl.semaphore_wait(late_in, HALF // 2)
 
     @pl.when(z == 0)

time: 32 us -> 32 us (level)
  no operation moved by 1% of the time
where the time goes in v4:
time: 32 us; the launch traced here: 31.8 us
  Pallas kernels  29.2 us (91%)
  between operations  1.31 us (4%)
  other arithmetic  1.29 us (4%)
    pallas_call x1, Pallas kernels, per_device(): pl.pallas_call(kernel, out_shape=jax.ShapeDtypeStruct((3, own_rows, width...  29.2 us
    convert_element_type x1, other arithmetic, per_device(): return (residual, (out[2] - residual / energy_gap).astype(jnp.bfloat16))  1.29 us

profile of v4, /device:TPU:1, one launch (start us, length us, event | category | flops | bytes accessed | tf_op | source)
XLA Modules:
  0.0 31.8 jit_solution(17998664584557578142)
XLA Ops:
  0.6 0.0 copy-start
  1.3 29.2 %shard_map.68 = f32[3,8,128]{2,1,0:T(8,128)} custom-call(s32[1,96]{1,0:T(1,128)} %bitcast.8, s32[1]{0:T(128)S(6)} %copy.7.dims_in, bf16[32,128]{1,0:T(8,128)(2,1)} %amplitudes.1, bf16[1,1,96,128,128]{4,3,2,1,0:T(8,128)(2,1)} %integrals.1), custom_call_target="tpu_custom_call" | custom-call | flops 100663296 | bytes 3145728 | tf_op jit(solution)/shard_map/pallas_call | solution.py:411
  30.5 0.0 copy-done
  30.5 1.3 %fusion = (bf16[8,128]{1,0:T(8,128)(2,1)}, f32[8,128]{1,0:T(8,128)}) fusion(f32[8,128]{1,0:T(8,128)S(1)} %copy-done, f32[3,8,128]{2,1,0:T(8,128)} %shard_map.68), kind=kLoop, calls=%fused_computation.1 | loop fusion | flops 4096 | bytes 22528 | tf_op jit(solution)/shard_map/convert_element_type | solution.py:456
Async XLA Ops:
  0.6 29.9 %copy-start = (f32[8,128]{1,0:T(8,128)S(1)}, f32[8,128]{1,0:T(8,128)}, u32[]{:S(2)}) copy-start(f32[8,128]{1,0:T(8,128)} %param.9) | copy-start | bytes 12292
